TPU v7x, 256 devices: a whole 4x4x8 slice. The times are simulated.
256 devices in a mesh: grp: 16 (over x_hi, z), blk: 16 (over x_lo, y, core).
Axes of the slice: x: 4 (x_hi: 2, x_lo: 2; x = x_hi * 2 + x_lo), y: 4, z: 8, core: 2. Of those that a mesh axis runs over, the one named last changes fastest.
Arguments:
- prompt_of: int32 [2048], P(('grp', 'blk')), may hold values from 0 to 31, as said below
- suffix_len: int32 [2048], P(('grp', 'blk')), may hold values from 1 to 256, as said below
- query: bfloat16 [2048, 4096], P(('grp', 'blk')), may hold values from -8 to 23
- new_key: bfloat16 [2048, 512], P(('grp', 'blk')), may hold values from -5 to 6
- new_value: bfloat16 [2048, 512], P(('grp', 'blk')), may hold values from -6 to 6
- suffix_key: bfloat16 [2048, 256, 512], P(('grp', 'blk')), may hold values from -5 to 6
- suffix_value: bfloat16 [2048, 256, 512], P(('grp', 'blk')), may hold values from -6 to 6
- prefix_key: bfloat16 [32, 4096, 512], P('grp', 'blk'), may hold values from -5 to 6
- prefix_value: bfloat16 [32, 4096, 512], P('grp', 'blk'), may hold values from -6 to 6
Outputs:
- attended: bfloat16 [2048, 4096], P(('grp', 'blk'))
Inputs may be any that keep to these rules, and one draw needn't show every extreme that they name: `prompt_of`: on every device at most 2 of its completions name prompts of one group (the group of a prompt is prompt // 2); one group gets exactly 2 from every device. `suffix_len`: some completion has exactly 256 cached suffix tokens.
All inputs are finite; a program needn't handle non-finite values.
Results may differ from a plain program's by a relative error of at most 0.0037.
Values may be sent and summed in bfloat16 or wider, within the bound.
No kernel may reach another device: no remote copies, remote signals or barrier semaphores. Data moves between devices by JAX's collectives and lax.ppermute only.
A program may use at most 128 MiB of HBM per device.

v0:
```python
import math

import jax
import jax.numpy as jnp
from jax import lax
from jax.experimental import pallas as pl
from jax.experimental.pallas import tpu as pltpu
from jax.sharding import Mesh, PartitionSpec as P

HD = 128
CAP = 2
HELD = 8
HEADS = 32
KVH = 4
RATIO = 8
PROMPTS = 32
SUF = 256
PIECE = 256
SLOTS = 256
ROWS = SLOTS * RATIO
NEG = -1e30
SCALE = HD ** (-0.5)
LOG2E = 1.4426950408889634
ALL = ("xh", "z", "xl", "y", "c")
NEAR = ("xl", "y")
FAR = ("xh", "z", "xl")


def slots_of(prompt_ref):
    prompts = [prompt_ref[i] for i in range(HELD)]
    slots = []
    for i in range(HELD):
        rank = jnp.int32(0)
        for j in range(i):
            rank = rank + jnp.where(prompts[j] == prompts[i], 1, 0)
        slots.append(prompts[i] * CAP + rank)
    return slots


def spread(values, index):
    picked = jnp.zeros(index.shape, jnp.int32)
    for i, value in enumerate(values):
        picked = jnp.where(index == i, value, picked)
    return picked


def prep_kernel(place_ref, prompt_hbm, query_hbm, key_ref, value_ref, *refs):
    send_refs = refs[:4]
    cut_refs = refs[4:12]
    prompt_ref, query_ref, small_sem, cut_sem = refs[12:]
    small = [
        pltpu.make_async_copy(prompt_hbm, prompt_ref, small_sem.at[0]),
        pltpu.make_async_copy(query_hbm, query_ref, small_sem.at[1]),
    ]
    for copy in small:
        copy.start()
    place = place_ref[0]
    copies = []
    for step, cut_ref in enumerate(cut_refs):
        target = place ^ step
        prompt = target >> 2
        column = pl.multiple_of((target & 3) * HD, HD)
        for n, cache in enumerate((key_ref, value_ref)):
            copies.append(
                pltpu.make_async_copy(
                    cache.at[prompt, :, pl.ds(column, HD)], cut_ref.at[n], cut_sem.at[step, n]
                )
            )
            copies[-1].start()
    for copy in small:
        copy.wait()
    slots = slots_of(prompt_ref)
    lane = lax.broadcasted_iota(jnp.int32, (HELD, HD), 1)
    row = lax.broadcasted_iota(jnp.int32, (HELD, HD), 0)
    tags = jnp.concatenate(
        [spread(slots, lane & 7).astype(jnp.float32), spread(slots, row).astype(jnp.float32)], axis=0
    ).astype(jnp.bfloat16)
    for step, send_ref in enumerate(send_refs):
        first = pl.multiple_of(((place & 3) ^ step) * RATIO * HD, RATIO * HD)
        mine = query_ref[:, pl.ds(first, RATIO * HD)].astype(jnp.float32)
        send_ref[:64] = jnp.concatenate(
            [mine[:, h * HD : (h + 1) * HD] for h in range(RATIO)], axis=0
        ).astype(jnp.bfloat16)
        send_ref[64:] = tags
    for copy in copies:
        copy.wait()


def sources_of(place_ref):
    return [(place_ref[0] & 3) ^ step for step in range(4)]


def pack_kernel(place_ref, *refs):
    got_refs = refs[:4]
    out_ref = refs[-1]
    sources = sources_of(place_ref)
    held = jnp.concatenate([got_ref[:64] for got_ref in got_refs], axis=0)
    tags = [got_ref[64:].astype(jnp.float32)[:1].astype(jnp.int32) for got_ref in got_refs]
    tags = [tags[s] + sources[s] * 512 for s in range(4)]
    half = lax.broadcasted_iota(jnp.int32, (1, HD), 1) < 64
    tag = jnp.concatenate([jnp.where(half, tags[0], tags[1]), jnp.where(half, tags[2], tags[3])], axis=1)
    lane_key = ((lax.broadcasted_iota(jnp.int32, (1, 256), 1) >> 3) & 7) * 64 + tag
    chunk = 512
    for start in range(0, ROWS, chunk):
        row = lax.broadcasted_iota(jnp.int32, (chunk, 1), 0) + start
        row_key = ((row >> 1) & 3) * 512 + ((row >> 3) & 7) * 64 + (row >> 6) * 2 + (row & 1)
        select = (row_key == lane_key).astype(jnp.float32).astype(jnp.bfloat16)
        out_ref[start : start + chunk, :] = jnp.dot(
            select, held, preferred_element_type=jnp.float32
        ).astype(jnp.bfloat16)


def near_kernel(
    len_ref, query_ref, new_key_ref, new_value_ref, key_ref, value_ref, out_ref, lse_ref, heads_ref
):
    step = pl.program_id(0)

    @pl.when(step == 0)
    def _():
        for h in range(HEADS):
            heads_ref[h] = query_ref[:, h * HD : (h + 1) * HD].astype(jnp.float32)

    length = len_ref[step]
    query = heads_ref[:, pl.ds(step, 1), :].reshape(HEADS, HD)
    keys = key_ref[0]
    values = value_ref[0]
    held_row = lax.broadcasted_iota(jnp.int32, (HELD, 1), 0)

    def row_of(ref):
        rows = jnp.where(held_row == step, ref[...].astype(jnp.float32), 0.0)
        return jnp.sum(rows, axis=0, keepdims=True)

    new_key = row_of(new_key_ref)
    new_value = row_of(new_value_ref)

    def spread_heads(row):
        return jnp.concatenate(
            [jnp.broadcast_to(row[:, k * HD : (k + 1) * HD], (RATIO, HD)) for k in range(KVH)], axis=0
        )

    scores = jnp.concatenate(
        [
            lax.dot_general(
                query.astype(jnp.bfloat16),
                keys[:, k * HD : (k + 1) * HD],
                (((1,), (1,)), ((), ())),
                preferred_element_type=jnp.float32,
            )[k * RATIO : (k + 1) * RATIO]
            for k in range(KVH)
        ],
        axis=0,
    ) * SCALE
    own = jnp.sum(query * spread_heads(new_key), axis=1, keepdims=True) * SCALE
    live = lax.broadcasted_iota(jnp.int32, (1, SUF), 1) < length
    scores = jnp.where(live, scores, NEG)
    top = jnp.maximum(jnp.max(scores, axis=1, keepdims=True), own)
    weights = jnp.where(live, jnp.exp(scores - top), 0.0)
    own_weight = jnp.exp(own - top)
    total = jnp.sum(weights, axis=1, keepdims=True) + own_weight
    rounded = weights.astype(jnp.bfloat16)
    mixed = jnp.concatenate(
        [
            jnp.dot(rounded, values[:, k * HD : (k + 1) * HD], preferred_element_type=jnp.float32)[
                k * RATIO : (k + 1) * RATIO
            ]
            for k in range(KVH)
        ],
        axis=0,
    )
    mixed = mixed + own_weight.astype(jnp.bfloat16).astype(jnp.float32) * spread_heads(new_value)
    out_ref[:, pl.ds(step, 1), :] = (mixed / total).reshape(HEADS, 1, HD)
    lse_ref[:, pl.ds(step, 1), :] = jnp.broadcast_to(top + jnp.log(total), (HEADS, HD)).reshape(
        HEADS, 1, HD
    )


def far_kernel(query_ref, *refs):
    pieces = refs[:16]
    out_ref, score_ref, query_scr, mixed_scr, stat_scr = refs[16:]
    span = 32
    block = span * RATIO
    tokens = 16 * PIECE
    queries = query_ref[...].astype(jnp.float32).reshape(32, RATIO, 8, HD)
    biggest = jnp.max(jnp.max(jnp.abs(queries), axis=1).reshape(SLOTS, HD), axis=1, keepdims=True)
    valid = (biggest > 0).astype(jnp.float32)
    row = lax.broadcasted_iota(jnp.int32, (SLOTS, SLOTS), 0)
    lane = lax.broadcasted_iota(jnp.int32, (SLOTS, SLOTS), 1)
    wide = jnp.broadcast_to(valid, (SLOTS, SLOTS)).astype(jnp.bfloat16)
    before = jnp.dot(
        (lane < row).astype(jnp.float32).astype(jnp.bfloat16), wide, preferred_element_type=jnp.float32
    )
    order = jnp.where(valid > 0, before, -1.0).astype(jnp.int32)
    gather = (order == lane).astype(jnp.float32).astype(jnp.bfloat16)
    count = jnp.sum(valid).astype(jnp.int32)
    for h in range(RATIO):
        query_scr[h] = lax.dot_general(
            gather,
            queries[:, h].reshape(SLOTS, HD).astype(jnp.bfloat16),
            (((0,), (0,)), ((), ())),
            preferred_element_type=jnp.float32,
        ).astype(jnp.bfloat16)
    mixed_scr[...] = jnp.zeros_like(mixed_scr)
    stat_scr[...] = jnp.zeros_like(stat_scr)

    @pl.loop(0, (count + span - 1) // span)
    def _(index):
        start = pl.multiple_of(index * span, span)
        query = query_scr[:, pl.ds(start, span), :].reshape(block, HD)
        peak = jnp.full((block, HD), -jnp.inf, jnp.float32)
        for n, piece in enumerate(pieces):
            scores = lax.dot_general(
                query, piece[0], (((1,), (1,)), ((), ())), preferred_element_type=jnp.float32
            )
            score_ref[n] = scores
            peak = jnp.maximum(peak, jnp.maximum(scores[:, :HD], scores[:, HD:]))
        peak = jnp.max(peak, axis=1, keepdims=True)
        total = jnp.zeros((block, HD), jnp.float32)
        mixed = jnp.zeros((block, HD), jnp.float32)
        for n, piece in enumerate(pieces):
            weights = jnp.exp2((score_ref[n] - peak) * (SCALE * LOG2E))
            total = total + (weights[:, :HD] + weights[:, HD:])
            mixed = mixed + jnp.dot(
                weights.astype(jnp.bfloat16), piece[1], preferred_element_type=jnp.float32
            )
        total = jnp.sum(total, axis=1, keepdims=True)
        mixed_scr[:, pl.ds(start, span), :] = (mixed / total).astype(jnp.bfloat16).reshape(RATIO, span, HD)
        lse = peak * SCALE + jnp.log(total)
        stat_scr[pl.ds(start, span), :] = split_stat(lse.reshape(RATIO, span, 1), span).astype(jnp.bfloat16)

    idle = 1.0 - valid
    mean = sum(piece[1].astype(jnp.float32).reshape(PIECE // 8, 8, HD).sum(axis=0) for piece in pieces)
    mean = jnp.sum(mean, axis=0, keepdims=True) / tokens
    heads = []
    for h in range(RATIO):
        spread_out = jnp.dot(gather, mixed_scr[h], preferred_element_type=jnp.float32) + idle * mean
        heads.append(spread_out.reshape(32, 8, HD))
    for h in range(0, RATIO, 2):
        out_ref[:, h * 8 : h * 8 + 16] = jnp.concatenate(heads[h : h + 2], axis=1).astype(jnp.bfloat16)
    even = split_stat(jnp.full((RATIO, SLOTS, 1), math.log(tokens), jnp.float32), SLOTS)
    stat = jnp.dot(gather, stat_scr[...], preferred_element_type=jnp.float32) + idle * even
    stat = stat.reshape(32, 8, HD)
    out_ref[:, 64:] = jnp.concatenate([stat, jnp.zeros_like(stat)], axis=1).astype(jnp.bfloat16)


def split_stat(lse, span):
    high = lse.astype(jnp.bfloat16).astype(jnp.float32)
    rest = lse - high
    middle = rest.astype(jnp.bfloat16).astype(jnp.float32)
    low = rest - middle
    lane = lax.broadcasted_iota(jnp.int32, (span, HD), 1)
    stat = jnp.zeros((span, HD), jnp.float32)
    for h in range(RATIO):
        for n, part in enumerate((high, middle, low)):
            stat = jnp.where(lane == n * 8 + h, part[h], stat)
    return stat


def select_kernel(place_ref, back_ref, *refs):
    got_refs = refs[:4]
    send_refs = refs[4:]
    sources = sources_of(place_ref)
    tags = [got_ref[64:].astype(jnp.float32)[8:, :1].astype(jnp.int32) for got_ref in got_refs]
    lane = lax.broadcasted_iota(jnp.int32, (1, ROWS), 1)
    lane_key = ((lane >> 1) & 3) * 512 + ((lane >> 3) & 7) * 64 + (lane >> 6) * 2 + (lane & 1)
    row_key = jnp.concatenate(
        [tags[s] + (sources[s] * 512 + h * 64) for s in range(4) for h in range(RATIO)], axis=0
    )
    select = (row_key == lane_key).astype(jnp.float32).astype(jnp.bfloat16)
    far = jnp.dot(select, back_ref[:, :64].reshape(ROWS, HD), preferred_element_type=jnp.float32)
    for s in range(4):
        send_refs[s][:64] = far[s * 64 : (s + 1) * 64].astype(jnp.bfloat16)
    stats = back_ref[:, 64:].astype(jnp.float32)[:, :8].reshape(SLOTS, HD).astype(jnp.bfloat16)
    lane = lax.broadcasted_iota(jnp.int32, (1, SLOTS), 1)
    lane_key = ((lane >> 1) & 3) * 64 + (lane >> 3) * 2 + (lane & 1)
    row_key = jnp.concatenate([tags[s] + sources[s] * 64 for s in range(4)], axis=0)
    select = (row_key == lane_key).astype(jnp.float32).astype(jnp.bfloat16)
    stat = jnp.dot(select, stats, preferred_element_type=jnp.float32)
    for s in range(4):
        mine = stat[s * 8 : (s + 1) * 8]
        send_refs[s][64:] = jnp.concatenate([mine, jnp.zeros_like(mine)], axis=0).astype(
            jnp.bfloat16
        )


def merge_kernel(place_ref, *refs):
    back_refs = refs[:4]
    near_ref, near_lse_ref, out_ref = refs[4:]
    lane = lax.broadcasted_iota(jnp.int32, (HELD, HD), 1)
    for source, back_ref in zip(sources_of(place_ref), back_refs):
        far = back_ref[:64].astype(jnp.float32)
        stat = jnp.where(lane < 24, back_ref[64:].astype(jnp.float32)[:8], 0.0)
        for h in range(RATIO):
            head = source * RATIO + h
            far_lse = jnp.sum(jnp.where((lane & 7) == h, stat, 0.0), axis=1, keepdims=True)
            near_lse = near_lse_ref[head]
            top = jnp.maximum(far_lse, near_lse)
            far_scale = jnp.exp(far_lse - top)
            near_scale = jnp.exp(near_lse - top)
            merged = far[h * 8 : (h + 1) * 8] * far_scale + near_ref[head] * near_scale
            out_ref[:, pl.ds(pl.multiple_of(head * HD, HD), HD)] = (
                merged / (far_scale + near_scale)
            ).astype(jnp.bfloat16)


VMEM = pl.BlockSpec(memory_space=pltpu.VMEM)
SMEM = pl.BlockSpec(memory_space=pltpu.SMEM)
ANY = pl.BlockSpec(memory_space=pl.ANY)


def params(mib):
    return pltpu.CompilerParams(vmem_limit_bytes=mib << 20)


def shards(
    prompt_of,
    suffix_len,
    query,
    new_key,
    new_value,
    suffix_key,
    suffix_value,
    prefix_key,
    prefix_value,
):
    place = lax.axis_index(NEAR).astype(jnp.int32).reshape(1)
    def along_y(pieces):
        moved = [lax.ppermute(pieces[step], "y", [(i, i ^ step) for i in range(4)]) for step in range(1, 4)]
        return [pieces[0]] + moved

    made = pl.pallas_call(
        prep_kernel,
        out_shape=[jax.ShapeDtypeStruct((80, HD), jnp.bfloat16)] * 4
        + [jax.ShapeDtypeStruct((2, PIECE, HD), jnp.bfloat16)] * 8,
        in_specs=[SMEM, ANY, ANY, ANY, ANY],
        out_specs=[VMEM] * 12,
        scratch_shapes=[
            pltpu.SMEM((HELD,), jnp.int32),
            pltpu.VMEM((HELD, HEADS * HD), jnp.bfloat16),
            pltpu.SemaphoreType.DMA((2,)),
            pltpu.SemaphoreType.DMA((8, 2)),
        ],
        compiler_params=params(12),
        name="prep",
    )(place, prompt_of, query, prefix_key, prefix_value)
    got = along_y(made[:4])
    cuts = made[4:]
    held = [cuts[0]]
    for step in range(1, 8):
        held.append(lax.ppermute(cuts[step], NEAR, [(i, i ^ step) for i in range(8)]))
    swapped = [lax.ppermute(piece, "c", [(0, 1), (1, 0)]) for piece in held]

    near_out, near_lse = pl.pallas_call(
        near_kernel,
        grid=(HELD,),
        out_shape=[jax.ShapeDtypeStruct((HEADS, HELD, HD), jnp.float32)] * 2,
        in_specs=[
            SMEM,
            pl.BlockSpec((HELD, HEADS * HD), lambda i: (0, 0)),
            pl.BlockSpec((HELD, KVH * HD), lambda i: (0, 0)),
            pl.BlockSpec((HELD, KVH * HD), lambda i: (0, 0)),
            pl.BlockSpec((1, SUF, KVH * HD), lambda i: (i, 0, 0)),
            pl.BlockSpec((1, SUF, KVH * HD), lambda i: (i, 0, 0)),
        ],
        out_specs=[pl.BlockSpec((HEADS, HELD, HD), lambda i: (0, 0, 0))] * 2,
        scratch_shapes=[pltpu.VMEM((HEADS, HELD, HD), jnp.float32)],
        compiler_params=params(12),
        cost_estimate=pl.CostEstimate(flops=300_000_000, bytes_accessed=4_500_000, transcendentals=65536),
        name="near",
    )(
        suffix_len,
        query,
        new_key,
        new_value,
        suffix_key,
        suffix_value,
    )

    first = held + swapped + [near_out, near_lse]
    outgoing = pl.pallas_call(
        pack_kernel,
        out_shape=jax.ShapeDtypeStruct((ROWS, HD), jnp.bfloat16),
        in_specs=[SMEM] + [VMEM] * 4 + [ANY] * len(first),
        out_specs=VMEM,
        compiler_params=params(8),
        name="pack",
    )(place, *got, *first)
    arrived = lax.all_to_all(outgoing.reshape(PROMPTS, 64, HD), FAR, 0, 0, tiled=True)

    parcel = pl.pallas_call(
        far_kernel,
        out_shape=jax.ShapeDtypeStruct((PROMPTS, 80, HD), jnp.bfloat16),
        in_specs=[VMEM] * 17,
        out_specs=VMEM,
        scratch_shapes=[
            pltpu.VMEM((16, 256, PIECE), jnp.float32),
            pltpu.VMEM((RATIO, SLOTS, HD), jnp.bfloat16),
            pltpu.VMEM((RATIO, SLOTS, HD), jnp.bfloat16),
            pltpu.VMEM((SLOTS, HD), jnp.bfloat16),
        ],
        compiler_params=params(16),
        name="far",
    )(arrived.reshape(ROWS, HD), *held, *swapped)
    back = lax.all_to_all(parcel, FAR, 0, 0, tiled=True)
    chosen = pl.pallas_call(
        select_kernel,
        out_shape=[jax.ShapeDtypeStruct((80, HD), jnp.bfloat16)] * 4,
        in_specs=[SMEM] + [VMEM] * 5,
        out_specs=[VMEM] * 4,
        compiler_params=params(8),
        name="select",
    )(place, back, *got)
    return pl.pallas_call(
        merge_kernel,
        out_shape=jax.ShapeDtypeStruct((HELD, HEADS * HD), jnp.bfloat16),
        in_specs=[SMEM] + [VMEM] * 6,
        out_specs=VMEM,
        compiler_params=params(12),
        name="merge",
    )(place, *along_y(chosen), near_out, near_lse)


def solution(mesh):
    fine = Mesh(mesh.devices.reshape(2, 8, 2, 4, 2), ALL)
    grp = ("xh", "z")
    blk = ("xl", "y", "c")
    in_specs = (
        P(ALL),
        P(ALL),
        P(ALL, None),
        P(ALL, None),
        P(ALL, None),
        P(ALL, None, None),
        P(ALL, None, None),
        P(grp, blk, None),
        P(grp, blk, None),
    )
    return jax.shard_map(
        shards, mesh=fine, in_specs=in_specs, out_specs=P(ALL, None), check_vma=False
    )
```

profile of v0, /device:TPU:32, one launch (start us, length us, event | category | flops | bytes accessed | tf_op | source)
XLA Modules:
  0.0 111.8 jit_solution(7606803481213381414)
XLA Ops:
  0.0 1.0 copy-done.2
  1.0 1.0 copy-done.3
  2.1 0.8 copy-done.4
  2.9 0.7 copy-done.8
  3.6 0.8 prep.1
  4.4 1.7 %collective-permute-start = (bf16[80,128]{1,0:T(8,128)(2,1)S(1)}, bf16[80,128]{1,0:T(8,128)(2,1)S(1)}, u32[]{:S(2)}, u32[]{:S(2)}) collective-permute-start(bf16[80,128]{1,0:T(8,128)(2,1)S(1)} %get-tuple-element.24), channel_id=1, source_target_pairs={{0,2},{2,0},{4,6},{6,4},{1,3},{3,1},{5,7},{7,5},{8,10},{10,8},{12,... | collective-permute-start | bytes 61448 | tf_op jit(solution)/shard_map/ppermute | solution.py:327
  6.0 2.9 %collective-permute-start.1 = (bf16[80,128]{1,0:T(8,128)(2,1)S(1)}, bf16[80,128]{1,0:T(8,128)(2,1)S(1)}, u32[]{:S(2)}, u32[]{:S(2)}) collective-permute-start(bf16[80,128]{1,0:T(8,128)(2,1)S(1)} %get-tuple-element.25), channel_id=1, source_target_pairs={{0,4},{2,6},{4,0},{6,2},{1,5},{3,7},{5,1},{7,3},{8,12},{10,14},{12... | collective-permute-start | bytes 61448 | tf_op jit(solution)/shard_map/ppermute | solution.py:327
  9.5 4.1 %collective-permute-start.4 = (bf16[2,256,128]{2,1,0:T(8,128)(2,1)S(1)}, bf16[2,256,128]{2,1,0:T(8,128)(2,1)S(1)}, u32[]{:S(2)}, u32[]{:S(2)}) collective-permute-start(bf16[2,256,128]{2,1,0:T(8,128)(2,1)S(1)} %get-tuple-element.29), channel_id=1, source_target_pairs={{0,4},{2,6},{4,0},{6,2},{8,12},{10,14},{12,8},{14,10},{1,5},{3,7},... | collective-permute-start | bytes 393224 | tf_op jit(solution)/shard_map/ppermute | solution.py:349
  13.9 1.5 %collective-permute-start.6 = (bf16[2,256,128]{2,1,0:T(8,128)(2,1)S(1)}, bf16[2,256,128]{2,1,0:T(8,128)(2,1)S(1)}, u32[]{:S(2)}, u32[]{:S(2)}) collective-permute-start(bf16[2,256,128]{2,1,0:T(8,128)(2,1)S(1)} %get-tuple-element.31), channel_id=1, source_target_pairs={{0,8},{2,10},{4,12},{6,14},{8,0},{10,2},{12,4},{14,6},{1,9},{3,11}... | collective-permute-start | bytes 393224 | tf_op jit(solution)/shard_map/ppermute | solution.py:349
  15.4 5.3 %collective-permute-start.8 = (bf16[2,256,128]{2,1,0:T(8,128)(2,1)S(1)}, bf16[2,256,128]{2,1,0:T(8,128)(2,1)S(1)}, u32[]{:S(2)}, u32[]{:S(2)}) collective-permute-start(bf16[2,256,128]{2,1,0:T(8,128)(2,1)S(1)} %get-tuple-element.33), channel_id=1, source_target_pairs={{0,12},{2,14},{4,8},{6,10},{8,4},{10,6},{12,0},{14,2},{1,13},{3,15... | collective-permute-start | bytes 393224 | tf_op jit(solution)/shard_map/ppermute | solution.py:349
  20.7 1.2 %collective-permute-start.9 = (bf16[2,256,128]{2,1,0:T(8,128)(2,1)S(1)}, bf16[2,256,128]{2,1,0:T(8,128)(2,1)S(1)}, u32[]{:S(2)}, u32[]{:S(2)}) collective-permute-start(bf16[2,256,128]{2,1,0:T(8,128)(2,1)S(1)} %get-tuple-element.34), channel_id=1, source_target_pairs={{0,14},{2,12},{4,10},{6,8},{8,6},{10,4},{12,2},{14,0},{1,15},{3,13... | collective-permute-start | bytes 393224 | tf_op jit(solution)/shard_map/ppermute | solution.py:349
  22.0 0.5 collective-permute-start.11
  22.7 4.1 %collective-permute-done.8.refs_10_.refs_6_ = bf16[2,256,128]{2,1,0:T(8,128)(2,1)S(1)} collective-permute-done((bf16[2,256,128]{2,1,0:T(8,128)(2,1)S(1)}, bf16[2,256,128]{2,1,0:T(8,128)(2,1)S(1)}, u32[]{:S(2)}, u32[]{:S(2)}) %collective-permute-start.8) | collective-permute-done | bytes 131104 | tf_op jit(solution)/shard_map/ppermute | solution.py:349
  26.8 1.5 %collective-permute-done.9.refs_11_.refs_7_ = bf16[2,256,128]{2,1,0:T(8,128)(2,1)S(1)} collective-permute-done((bf16[2,256,128]{2,1,0:T(8,128)(2,1)S(1)}, bf16[2,256,128]{2,1,0:T(8,128)(2,1)S(1)}, u32[]{:S(2)}, u32[]{:S(2)}) %collective-permute-start.9) | collective-permute-done | bytes 131104 | tf_op jit(solution)/shard_map/ppermute | solution.py:349
  28.3 0.5 collective-permute-start.15
  29.3 1.6 %copy-done = bf16[8,256,512]{2,1,0:T(8,128)(2,1)S(1)} copy-done((bf16[8,256,512]{2,1,0:T(8,128)(2,1)S(1)}, bf16[8,256,512]{2,1,0:T(8,128)(2,1)}, u32[]{:S(2)}) %copy-start) | copy-done | bytes 2097176
  30.9 1.6 %copy-done.1 = bf16[8,256,512]{2,1,0:T(8,128)(2,1)S(1)} copy-done((bf16[8,256,512]{2,1,0:T(8,128)(2,1)S(1)}, bf16[8,256,512]{2,1,0:T(8,128)(2,1)}, u32[]{:S(2)}) %copy-start.1) | copy-done | bytes 2097176
  32.5 0.8 copy-done.5
  33.3 0.7 copy-done.6
  34.0 0.7 copy-done.7
  34.7 0.7 copy-done.9
  35.4 4.0 %near.1 = (f32[32,8,128]{2,1,0:T(8,128)S(1)}, f32[32,8,128]{2,1,0:T(8,128)S(1)}) custom-call(s32[8]{0:T(128)S(1)} %copy-done.9, bf16[8,4096]{1,0:T(8,128)(2,1)S(1)} %copy-done.5, bf16[8,512]{1,0:T(8,128)(2,1)S(1)} %copy-done.6, bf16[8,512]{1,0:T(8,128)(2,1)S(1)} %copy-done.7, bf16[8,256,512]{2,1,0:T(8,128)(2,1)S(1)} %copy-done, ...), custom_call_target="tpu_custom_call" | custom-call | flops 300000000 | bytes 4500000 | tf_op jit(solution)/shard_map/near/pallas_call | solution.py:352
  39.5 0.7 pack.1
  40.1 29.6 %all_to_all.10 = bf16[32,64,128]{2,1,0:T(8,128)(2,1)S(1)} all-to-all(bf16[32,64,128]{2,1,0:T(8,128)(2,1)S(1)} %bitcast.4), channel_id=1, replica_groups=mesh['xh'=2,'z'=8,'xl'=2,'y'=4,'c'=2] {'xh','z','xl'}, dimensions={0} | all-to-all | bytes 1048576 | tf_op jit(solution)/shard_map/all_to_all | solution.py:387
  69.8 5.2 %far.1 = bf16[32,80,128]{2,1,0:T(8,128)(2,1)S(1)} custom-call(bf16[2048,128]{1,0:T(8,128)(2,1)S(1)} %bitcast.3, bf16[2,256,128]{2,1,0:T(8,128)(2,1)S(1)} %get-tuple-element.27.refs_4_.refs_0_, bf16[2,256,128]{2,1,0:T(8,128)(2,1)S(1)} %collective-permute-done.3.refs_5_.refs_1_, bf16[2,256,128]{2,1,0:T(8,128)(2,1)S(1)} %collective-permute-done.4.refs_6_.refs_2_, ...), custom_call_target="tpu_custom_call" | custom-call | tf_op jit(solution)/shard_map/far/pallas_call | solution.py:389
  75.0 28.3 %all_to_all.11.back_ref = bf16[32,80,128]{2,1,0:T(8,128)(2,1)S(1)} all-to-all(bf16[32,80,128]{2,1,0:T(8,128)(2,1)S(1)} %far.1), channel_id=1, replica_groups=mesh['xh'=2,'z'=8,'xl'=2,'y'=4,'c'=2] {'xh','z','xl'}, dimensions={0} | all-to-all | bytes 1310720 | tf_op jit(solution)/shard_map/all_to_all | solution.py:403
  103.8 1.3 %collective-permute-start.18 = (bf16[80,128]{1,0:T(8,128)(2,1)S(1)}, bf16[80,128]{1,0:T(8,128)(2,1)S(1)}, u32[]{:S(2)}, u32[]{:S(2)}) collective-permute-start(bf16[80,128]{1,0:T(8,128)(2,1)S(1)} %get-tuple-element.38), channel_id=1, source_target_pairs={{0,2},{2,0},{4,6},{6,4},{1,3},{3,1},{5,7},{7,5},{8,10},{10,8},{12,... | collective-permute-start | bytes 61448 | tf_op jit(solution)/shard_map/ppermute | solution.py:327
  105.0 1.0 collective-permute-start.19
  106.0 2.5 %collective-permute-start.20 = (bf16[80,128]{1,0:T(8,128)(2,1)S(1)}, bf16[80,128]{1,0:T(8,128)(2,1)S(1)}, u32[]{:S(2)}, u32[]{:S(2)}) collective-permute-start(bf16[80,128]{1,0:T(8,128)(2,1)S(1)} %get-tuple-element.40), channel_id=1, source_target_pairs={{0,6},{2,4},{4,2},{6,0},{1,7},{3,5},{5,3},{7,1},{8,14},{10,12},{12... | collective-permute-start | bytes 61448 | tf_op jit(solution)/shard_map/ppermute | solution.py:327
  108.5 1.8 %collective-permute-done.19.refs_2_ = bf16[80,128]{1,0:T(8,128)(2,1)S(1)} collective-permute-done((bf16[80,128]{1,0:T(8,128)(2,1)S(1)}, bf16[80,128]{1,0:T(8,128)(2,1)S(1)}, u32[]{:S(2)}, u32[]{:S(2)}) %collective-permute-start.19) | collective-permute-done | bytes 20512 | tf_op jit(solution)/shard_map/ppermute | solution.py:327
  110.3 0.7 collective-permute-done.20.refs_3_
  111.0 0.8 merge.1
  (38 shorter events, 2.1 us)
Async XLA Ops:
  0.0 1.0 copy-start.2
  1.0 1.0 copy-start.3
  2.1 0.8 copy-start.4
  2.9 0.7 copy-start.8
  4.4 9.3 %collective-permute-start = (bf16[80,128]{1,0:T(8,128)(2,1)S(1)}, bf16[80,128]{1,0:T(8,128)(2,1)S(1)}, u32[]{:S(2)}, u32[]{:S(2)}) collective-permute-start(bf16[80,128]{1,0:T(8,128)(2,1)S(1)} %get-tuple-element.24), channel_id=1, source_target_pairs={{0,2},{2,0},{4,6},{6,4},{1,3},{3,1},{5,7},{7,5},{8,10},{10,8},{12,... | collective-permute-start | bytes 61448 | tf_op jit(solution)/shard_map/ppermute | solution.py:327
  6.0 7.8 %collective-permute-start.1 = (bf16[80,128]{1,0:T(8,128)(2,1)S(1)}, bf16[80,128]{1,0:T(8,128)(2,1)S(1)}, u32[]{:S(2)}, u32[]{:S(2)}) collective-permute-start(bf16[80,128]{1,0:T(8,128)(2,1)S(1)} %get-tuple-element.25), channel_id=1, source_target_pairs={{0,4},{2,6},{4,0},{6,2},{1,5},{3,7},{5,1},{7,3},{8,12},{10,14},{12... | collective-permute-start | bytes 61448 | tf_op jit(solution)/shard_map/ppermute | solution.py:327
  8.9 6.4 %collective-permute-start.2 = (bf16[80,128]{1,0:T(8,128)(2,1)S(1)}, bf16[80,128]{1,0:T(8,128)(2,1)S(1)}, u32[]{:S(2)}, u32[]{:S(2)}) collective-permute-start(bf16[80,128]{1,0:T(8,128)(2,1)S(1)} %get-tuple-element.26), channel_id=1, source_target_pairs={{0,6},{2,4},{4,2},{6,0},{1,7},{3,5},{5,3},{7,1},{8,14},{10,12},{12... | collective-permute-start | bytes 61448 | tf_op jit(solution)/shard_map/ppermute | solution.py:327
  9.1 6.2 %collective-permute-start.3 = (bf16[2,256,128]{2,1,0:T(8,128)(2,1)S(1)}, bf16[2,256,128]{2,1,0:T(8,128)(2,1)S(1)}, u32[]{:S(2)}, u32[]{:S(2)}) collective-permute-start(bf16[2,256,128]{2,1,0:T(8,128)(2,1)S(1)} %get-tuple-element.28), channel_id=1, source_target_pairs={{0,2},{2,0},{4,6},{6,4},{8,10},{10,8},{12,14},{14,12},{1,3},{3,1},... | collective-permute-start | bytes 393224 | tf_op jit(solution)/shard_map/ppermute | solution.py:349
  9.5 11.2 %collective-permute-start.4 = (bf16[2,256,128]{2,1,0:T(8,128)(2,1)S(1)}, bf16[2,256,128]{2,1,0:T(8,128)(2,1)S(1)}, u32[]{:S(2)}, u32[]{:S(2)}) collective-permute-start(bf16[2,256,128]{2,1,0:T(8,128)(2,1)S(1)} %get-tuple-element.29), channel_id=1, source_target_pairs={{0,4},{2,6},{4,0},{6,2},{8,12},{10,14},{12,8},{14,10},{1,5},{3,7},... | collective-permute-start | bytes 393224 | tf_op jit(solution)/shard_map/ppermute | solution.py:349
  13.6 8.3 %collective-permute-start.5 = (bf16[2,256,128]{2,1,0:T(8,128)(2,1)S(1)}, bf16[2,256,128]{2,1,0:T(8,128)(2,1)S(1)}, u32[]{:S(2)}, u32[]{:S(2)}) collective-permute-start(bf16[2,256,128]{2,1,0:T(8,128)(2,1)S(1)} %get-tuple-element.30), channel_id=1, source_target_pairs={{0,6},{2,4},{4,2},{6,0},{8,14},{10,12},{12,10},{14,8},{1,7},{3,5},... | collective-permute-start | bytes 393224 | tf_op jit(solution)/shard_map/ppermute | solution.py:349
  13.9 8.1 %collective-permute-start.6 = (bf16[2,256,128]{2,1,0:T(8,128)(2,1)S(1)}, bf16[2,256,128]{2,1,0:T(8,128)(2,1)S(1)}, u32[]{:S(2)}, u32[]{:S(2)}) collective-permute-start(bf16[2,256,128]{2,1,0:T(8,128)(2,1)S(1)} %get-tuple-element.31), channel_id=1, source_target_pairs={{0,8},{2,10},{4,12},{6,14},{8,0},{10,2},{12,4},{14,6},{1,9},{3,11}... | collective-permute-start | bytes 393224 | tf_op jit(solution)/shard_map/ppermute | solution.py:349
  15.3 7.3 %collective-permute-start.7 = (bf16[2,256,128]{2,1,0:T(8,128)(2,1)S(1)}, bf16[2,256,128]{2,1,0:T(8,128)(2,1)S(1)}, u32[]{:S(2)}, u32[]{:S(2)}) collective-permute-start(bf16[2,256,128]{2,1,0:T(8,128)(2,1)S(1)} %get-tuple-element.32), channel_id=1, source_target_pairs={{0,10},{2,8},{4,14},{6,12},{8,2},{10,0},{12,6},{14,4},{1,11},{3,9}... | collective-permute-start | bytes 393224 | tf_op jit(solution)/shard_map/ppermute | solution.py:349
  15.4 11.4 %collective-permute-start.8 = (bf16[2,256,128]{2,1,0:T(8,128)(2,1)S(1)}, bf16[2,256,128]{2,1,0:T(8,128)(2,1)S(1)}, u32[]{:S(2)}, u32[]{:S(2)}) collective-permute-start(bf16[2,256,128]{2,1,0:T(8,128)(2,1)S(1)} %get-tuple-element.33), channel_id=1, source_target_pairs={{0,12},{2,14},{4,8},{6,10},{8,4},{10,6},{12,0},{14,2},{1,13},{3,15... | collective-permute-start | bytes 393224 | tf_op jit(solution)/shard_map/ppermute | solution.py:349
  20.7 7.6 %collective-permute-start.9 = (bf16[2,256,128]{2,1,0:T(8,128)(2,1)S(1)}, bf16[2,256,128]{2,1,0:T(8,128)(2,1)S(1)}, u32[]{:S(2)}, u32[]{:S(2)}) collective-permute-start(bf16[2,256,128]{2,1,0:T(8,128)(2,1)S(1)} %get-tuple-element.34), channel_id=1, source_target_pairs={{0,14},{2,12},{4,10},{6,8},{8,6},{10,4},{12,2},{14,0},{1,15},{3,13... | collective-permute-start | bytes 393224 | tf_op jit(solution)/shard_map/ppermute | solution.py:349
  21.9 6.4 %collective-permute-start.10 = (bf16[2,256,128]{2,1,0:T(8,128)(2,1)S(1)}, bf16[2,256,128]{2,1,0:T(8,128)(2,1)S(1)}, u32[]{:S(2)}, u32[]{:S(2)}) collective-permute-start(bf16[2,256,128]{2,1,0:T(8,128)(2,1)S(1)} %get-tuple-element.27.refs_4_.refs_0_), channel_id=1, source_target_pairs={{0,1},{1,0},{2,3},{3,2},{4,5},{5,4},{6,7},{7,6},{8,9},{9,8},{10,11... | collective-permute-start | bytes 393224 | tf_op jit(solution)/shard_map/ppermute | solution.py:350
  22.0 6.9 %collective-permute-start.11 = (bf16[2,256,128]{2,1,0:T(8,128)(2,1)S(1)}, bf16[2,256,128]{2,1,0:T(8,128)(2,1)S(1)}, u32[]{:S(2)}, u32[]{:S(2)}) collective-permute-start(bf16[2,256,128]{2,1,0:T(8,128)(2,1)S(1)} %collective-permute-done.3.refs_5_.refs_1_), channel_id=1, source_target_pairs={{0,1},{1,0},{2,3},{3,2},{4,5},{5,4},{6,7},{7,6},{8,9},{9,8},{10,11... | collective-permute-start | bytes 393224 | tf_op jit(solution)/shard_map/ppermute | solution.py:350
  22.7 6.2 %collective-permute-start.12 = (bf16[2,256,128]{2,1,0:T(8,128)(2,1)S(1)}, bf16[2,256,128]{2,1,0:T(8,128)(2,1)S(1)}, u32[]{:S(2)}, u32[]{:S(2)}) collective-permute-start(bf16[2,256,128]{2,1,0:T(8,128)(2,1)S(1)} %collective-permute-done.4.refs_6_.refs_2_), channel_id=1, source_target_pairs={{0,1},{1,0},{2,3},{3,2},{4,5},{5,4},{6,7},{7,6},{8,9},{9,8},{10,11... | collective-permute-start | bytes 393224 | tf_op jit(solution)/shard_map/ppermute | solution.py:350
  26.8 12.6 %collective-permute-start.13 = (bf16[2,256,128]{2,1,0:T(8,128)(2,1)S(1)}, bf16[2,256,128]{2,1,0:T(8,128)(2,1)S(1)}, u32[]{:S(2)}, u32[]{:S(2)}) collective-permute-start(bf16[2,256,128]{2,1,0:T(8,128)(2,1)S(1)} %collective-permute-done.5.refs_7_.refs_3_), channel_id=1, source_target_pairs={{0,1},{1,0},{2,3},{3,2},{4,5},{5,4},{6,7},{7,6},{8,9},{9,8},{10,11... | collective-permute-start | bytes 393224 | tf_op jit(solution)/shard_map/ppermute | solution.py:350
  28.3 11.1 %collective-permute-start.14 = (bf16[2,256,128]{2,1,0:T(8,128)(2,1)S(1)}, bf16[2,256,128]{2,1,0:T(8,128)(2,1)S(1)}, u32[]{:S(2)}, u32[]{:S(2)}) collective-permute-start(bf16[2,256,128]{2,1,0:T(8,128)(2,1)S(1)} %collective-permute-done.6.refs_8_.refs_4_), channel_id=1, source_target_pairs={{0,1},{1,0},{2,3},{3,2},{4,5},{5,4},{6,7},{7,6},{8,9},{9,8},{10,11... | collective-permute-start | bytes 393224 | tf_op jit(solution)/shard_map/ppermute | solution.py:350
  28.3 11.1 %collective-permute-start.15 = (bf16[2,256,128]{2,1,0:T(8,128)(2,1)S(1)}, bf16[2,256,128]{2,1,0:T(8,128)(2,1)S(1)}, u32[]{:S(2)}, u32[]{:S(2)}) collective-permute-start(bf16[2,256,128]{2,1,0:T(8,128)(2,1)S(1)} %collective-permute-done.7.refs_9_.refs_5_), channel_id=1, source_target_pairs={{0,1},{1,0},{2,3},{3,2},{4,5},{5,4},{6,7},{7,6},{8,9},{9,8},{10,11... | collective-permute-start | bytes 393224 | tf_op jit(solution)/shard_map/ppermute | solution.py:350
  28.8 10.6 %collective-permute-start.16 = (bf16[2,256,128]{2,1,0:T(8,128)(2,1)S(1)}, bf16[2,256,128]{2,1,0:T(8,128)(2,1)S(1)}, u32[]{:S(2)}, u32[]{:S(2)}) collective-permute-start(bf16[2,256,128]{2,1,0:T(8,128)(2,1)S(1)} %collective-permute-done.8.refs_10_.refs_6_), channel_id=1, source_target_pairs={{0,1},{1,0},{2,3},{3,2},{4,5},{5,4},{6,7},{7,6},{8,9},{9,8},{10,11... | collective-permute-start | bytes 393224 | tf_op jit(solution)/shard_map/ppermute | solution.py:350
  28.9 10.5 %collective-permute-start.17 = (bf16[2,256,128]{2,1,0:T(8,128)(2,1)S(1)}, bf16[2,256,128]{2,1,0:T(8,128)(2,1)S(1)}, u32[]{:S(2)}, u32[]{:S(2)}) collective-permute-start(bf16[2,256,128]{2,1,0:T(8,128)(2,1)S(1)} %collective-permute-done.9.refs_11_.refs_7_), channel_id=1, source_target_pairs={{0,1},{1,0},{2,3},{3,2},{4,5},{5,4},{6,7},{7,6},{8,9},{9,8},{10,11... | collective-permute-start | bytes 393224 | tf_op jit(solution)/shard_map/ppermute | solution.py:350
  29.3 1.6 %copy-start = (bf16[8,256,512]{2,1,0:T(8,128)(2,1)S(1)}, bf16[8,256,512]{2,1,0:T(8,128)(2,1)}, u32[]{:S(2)}) copy-start(bf16[8,256,512]{2,1,0:T(8,128)(2,1)} %key_ref.3) | copy-start | bytes 6291460
  30.9 1.6 %copy-start.1 = (bf16[8,256,512]{2,1,0:T(8,128)(2,1)S(1)}, bf16[8,256,512]{2,1,0:T(8,128)(2,1)}, u32[]{:S(2)}) copy-start(bf16[8,256,512]{2,1,0:T(8,128)(2,1)} %value_ref.3) | copy-start | bytes 6291460
  32.5 0.8 copy-start.5
  33.3 0.7 copy-start.6
  34.0 0.7 copy-start.7
  34.7 0.7 copy-start.9
  103.8 4.8 %collective-permute-start.18 = (bf16[80,128]{1,0:T(8,128)(2,1)S(1)}, bf16[80,128]{1,0:T(8,128)(2,1)S(1)}, u32[]{:S(2)}, u32[]{:S(2)}) collective-permute-start(bf16[80,128]{1,0:T(8,128)(2,1)S(1)} %get-tuple-element.38), channel_id=1, source_target_pairs={{0,2},{2,0},{4,6},{6,4},{1,3},{3,1},{5,7},{7,5},{8,10},{10,8},{12,... | collective-permute-start | bytes 61448 | tf_op jit(solution)/shard_map/ppermute | solution.py:327
  105.0 5.3 %collective-permute-start.19 = (bf16[80,128]{1,0:T(8,128)(2,1)S(1)}, bf16[80,128]{1,0:T(8,128)(2,1)S(1)}, u32[]{:S(2)}, u32[]{:S(2)}) collective-permute-start(bf16[80,128]{1,0:T(8,128)(2,1)S(1)} %get-tuple-element.39), channel_id=1, source_target_pairs={{0,4},{2,6},{4,0},{6,2},{1,5},{3,7},{5,1},{7,3},{8,12},{10,14},{12... | collective-permute-start | bytes 61448 | tf_op jit(solution)/shard_map/ppermute | solution.py:327
  106.0 5.0 %collective-permute-start.20 = (bf16[80,128]{1,0:T(8,128)(2,1)S(1)}, bf16[80,128]{1,0:T(8,128)(2,1)S(1)}, u32[]{:S(2)}, u32[]{:S(2)}) collective-permute-start(bf16[80,128]{1,0:T(8,128)(2,1)S(1)} %get-tuple-element.40), channel_id=1, source_target_pairs={{0,6},{2,4},{4,2},{6,0},{1,7},{3,5},{5,3},{7,1},{8,14},{10,12},{12... | collective-permute-start | bytes 61448 | tf_op jit(solution)/shard_map/ppermute | solution.py:327
where the time goes:
time: 112 us
  blocking collectives  57.9 us (52%)
  starting transfers between devices  23.8 us (21%)
  Pallas kernels  11.9 us (11%)
  local copies, waits for them, and re-layouts  9.64 us (9%)
  waiting for transfers between devices  8.37 us (7%)
    all_to_all x1, blocking collectives, shards(): lax.all_to_all(outgoing.reshape(PROMPTS, 64, HD), FAR, 0, 0, tiled=True)  29.6 us
    all_to_all x1, blocking collectives, shards(): back = lax.all_to_all(parcel, FAR, 0, 0, tiled=True)  28.3 us
    ppermute x7, starting transfers between devices, shards(): lax.ppermute(cuts[step], NEAR, [(i, i ^ step) for i in range(8)])  12.7 us
    unnamed x20, local copies, waits for them, and re-layouts  9.64 us
    ppermute x6, starting transfers between devices, along_y(): lax.ppermute(pieces[step], 'y', [(i, i ^ step) for i in range(4)])  9.57 us
    ppermute x7, waiting for transfers between devices, shards(): lax.ppermute(cuts[step], NEAR, [(i, i ^ step) for i in range(8)])  5.87 us
    pallas_call x1, Pallas kernels, shards(): pl.pallas_call(far_kernel, out_shape=jax.ShapeDtypeStruct((PROMPTS, 80, H...  5.19 us
    pallas_call x1, Pallas kernels, shards(): pl.pallas_call(near_kernel, grid=(HELD,), out_shape=[jax.ShapeDtypeStruct...  4 us
  transfers between devices with their start and end apart: 21, of which 5 were waited for; matrix products, arithmetic and copies ran while one was open for 0% of the time, Pallas kernels for 4%

commit v1 on v0

--- a/solution.py
+++ b/solution.py
@@ -175,8 +175,15 @@
 
 
 def far_kernel(query_ref, *refs):
-    pieces = refs[:16]
-    out_ref, score_ref, query_scr, mixed_scr, stat_scr = refs[16:]
+    sources = refs[:16]
+    out_ref, score_ref, query_scr, mixed_scr, stat_scr, cache_ref, sems = refs[16:]
+    copies = [
+        [pltpu.make_async_copy(source.at[k], cache_ref.at[n, k], sems.at[n, k]) for n, source in enumerate(sources)]
+        for k in range(2)
+    ]
+    for copy in copies[0] + copies[1]:
+        copy.start()
+    pieces = [cache_ref.at[n] for n in range(16)]
     span = 32
     block = span * RATIO
     tokens = 16 * PIECE
@@ -201,6 +208,8 @@
         ).astype(jnp.bfloat16)
     mixed_scr[...] = jnp.zeros_like(mixed_scr)
     stat_scr[...] = jnp.zeros_like(stat_scr)
+    for copy in copies[0]:
+        copy.wait()
 
     @pl.loop(0, (count + span - 1) // span)
     def _(index):
@@ -214,6 +223,12 @@
             score_ref[n] = scores
             peak = jnp.maximum(peak, jnp.maximum(scores[:, :HD], scores[:, HD:]))
         peak = jnp.max(peak, axis=1, keepdims=True)
+
+        @pl.when(index == 0)
+        def _():
+            for copy in copies[1]:
+                copy.wait()
+
         total = jnp.zeros((block, HD), jnp.float32)
         mixed = jnp.zeros((block, HD), jnp.float32)
         for n, piece in enumerate(pieces):
@@ -226,6 +241,11 @@
         mixed_scr[:, pl.ds(start, span), :] = (mixed / total).astype(jnp.bfloat16).reshape(RATIO, span, HD)
         lse = peak * SCALE + jnp.log(total)
         stat_scr[pl.ds(start, span), :] = split_stat(lse.reshape(RATIO, span, 1), span).astype(jnp.bfloat16)
+
+    @pl.when(count == 0)
+    def _():
+        for copy in copies[1]:
+            copy.wait()
 
     idle = 1.0 - valid
     mean = sum(piece[1].astype(jnp.float32).reshape(PIECE // 8, 8, HD).sum(axis=0) for piece in pieces)
@@ -257,7 +277,7 @@
 
 def select_kernel(place_ref, back_ref, *refs):
     got_refs = refs[:4]
-    send_refs = refs[4:]
+    send_refs = refs[-4:]
     sources = sources_of(place_ref)
     tags = [got_ref[64:].astype(jnp.float32)[8:, :1].astype(jnp.int32) for got_ref in got_refs]
     lane = lax.broadcasted_iota(jnp.int32, (1, ROWS), 1)
@@ -339,7 +359,7 @@
             pltpu.SemaphoreType.DMA((2,)),
             pltpu.SemaphoreType.DMA((8, 2)),
         ],
-        compiler_params=params(12),
+        compiler_params=params(60),
         name="prep",
     )(place, prompt_of, query, prefix_key, prefix_value)
     got = along_y(made[:4])
@@ -375,7 +395,7 @@
         suffix_value,
     )
 
-    first = held + swapped + [near_out, near_lse]
+    first = held[4:]
     outgoing = pl.pallas_call(
         pack_kernel,
         out_shape=jax.ShapeDtypeStruct((ROWS, HD), jnp.bfloat16),
@@ -389,26 +409,28 @@
     parcel = pl.pallas_call(
         far_kernel,
         out_shape=jax.ShapeDtypeStruct((PROMPTS, 80, HD), jnp.bfloat16),
-        in_specs=[VMEM] * 17,
+        in_specs=[VMEM] + [ANY] * 16,
         out_specs=VMEM,
         scratch_shapes=[
             pltpu.VMEM((16, 256, PIECE), jnp.float32),
             pltpu.VMEM((RATIO, SLOTS, HD), jnp.bfloat16),
             pltpu.VMEM((RATIO, SLOTS, HD), jnp.bfloat16),
             pltpu.VMEM((SLOTS, HD), jnp.bfloat16),
+            pltpu.VMEM((16, 2, PIECE, HD), jnp.bfloat16),
+            pltpu.SemaphoreType.DMA((16, 2)),
         ],
-        compiler_params=params(16),
+        compiler_params=params(60),
         name="far",
     )(arrived.reshape(ROWS, HD), *held, *swapped)
     back = lax.all_to_all(parcel, FAR, 0, 0, tiled=True)
     chosen = pl.pallas_call(
         select_kernel,
         out_shape=[jax.ShapeDtypeStruct((80, HD), jnp.bfloat16)] * 4,
-        in_specs=[SMEM] + [VMEM] * 5,
+        in_specs=[SMEM] + [VMEM] * 5 + [ANY] * 2,
         out_specs=[VMEM] * 4,
         compiler_params=params(8),
         name="select",
-    )(place, back, *got)
+    )(place, back, *got, near_out, near_lse)
     return pl.pallas_call(
         merge_kernel,
         out_shape=jax.ShapeDtypeStruct((HELD, HEADS * HD), jnp.bfloat16),

time: 112 us -> 101 us (0.902)
  blocking collectives: 57.9 us -> 0 us
  waiting for transfers between devices: 8.37 us -> 35.8 us
  starting transfers between devices: 23.8 us -> 45 us
  local copies, waits for them, and re-layouts: 9.64 us -> 3.18 us
  Pallas kernels: 11.9 us -> 15.5 us
    all_to_all x2 -> x0, blocking collectives: 57.9 us -> none  [the longest x1 29.6 us: shards(): lax.all_to_all(outgoing.reshape(PROMPTS, 64, HD), FAR, 0, 0, tiled=True)]
    all_to_all x0 -> x2, starting transfers between devices: none -> 20.9 us  [the longest x1 11.2 us: shards(): lax.all_to_all(outgoing.reshape(PROMPTS, 64, HD), FAR, 0, 0, tiled=True)]
    all_to_all x0 -> x2, waiting for transfers between devices: none -> 17.7 us  [the longest x1 13.7 us: shards(): back = lax.all_to_all(parcel, FAR, 0, 0, tiled=True)]
    ppermute x6, waiting for transfers between devices: 2.47 us -> 12.1 us  [along_y(): lax.ppermute(pieces[step], 'y', [(i, i ^ step) for i in range(4)])]
    unnamed x20 -> x56, local copies, waits for them, and re-layouts: 9.64 us -> 3.18 us
    pallas_call x1, Pallas kernels: 0.77 us -> 2.44 us  [shards(): pl.pallas_call(prep_kernel, out_shape=[jax.ShapeDtypeStruct((80, HD), jnp...]
  transfers between devices with their start and end apart: 21 -> 23, of which waited for: 5 -> 13; matrix products, arithmetic and copies ran while one was open for 0% -> 0% of each run, Pallas kernels for 4% -> 4%
where the time goes in v1:
time: 101 us; the launch traced here: 99.8 us
  starting transfers between devices  45 us (45%)
  waiting for transfers between devices  35.8 us (35%)
  Pallas kernels  15.5 us (15%)
  local copies, waits for them, and re-layouts  3.18 us (3%)
    all_to_all x1, waiting for transfers between devices, shards(): back = lax.all_to_all(parcel, FAR, 0, 0, tiled=True)  13.7 us
    ppermute x6, waiting for transfers between devices, along_y(): lax.ppermute(pieces[step], 'y', [(i, i ^ step) for i in range(4)])  12.1 us
    ppermute x7, starting transfers between devices, shards(): lax.ppermute(cuts[step], NEAR, [(i, i ^ step) for i in range(8)])  11.9 us
    all_to_all x1, starting transfers between devices, shards(): lax.all_to_all(outgoing.reshape(PROMPTS, 64, HD), FAR, 0, 0, tiled=True)  11.2 us
    ppermute x6, starting transfers between devices, along_y(): lax.ppermute(pieces[step], 'y', [(i, i ^ step) for i in range(4)])  10.6 us
    all_to_all x1, starting transfers between devices, shards(): back = lax.all_to_all(parcel, FAR, 0, 0, tiled=True)  9.73 us
    pallas_call x1, Pallas kernels, shards(): pl.pallas_call(far_kernel, out_shape=jax.ShapeDtypeStruct((PROMPTS, 80, H...  6.26 us
    ppermute x7, waiting for transfers between devices, shards(): lax.ppermute(cuts[step], NEAR, [(i, i ^ step) for i in range(8)])  4.87 us
  transfers between devices with their start and end apart: 23, of which 13 were waited for; matrix products, arithmetic and copies ran while one was open for 0% of the time, Pallas kernels for 4%

profile of v1, /device:TPU:32, one launch (start us, length us, event | category | flops | bytes accessed | tf_op | source)
XLA Modules:
  0.0 99.8 jit_solution(3676910114785155015)
XLA Ops:
  0.0 2.4 %prep.1 = (bf16[80,128]{1,0:T(8,128)(2,1)}, bf16[80,128]{1,0:T(8,128)(2,1)}, bf16[80,128]{1,0:T(8,128)(2,1)}, bf16[80,128]{1,0:T(8,128)(2,1)}, bf16[2,256,128]{2...) custom-call(s32[1]{0:T(128)} %bitcast.place_ref, ...), custom_call_target="tpu_custom_call" | custom-call | tf_op jit(solution)/shard_map/prep/pallas_call | solution.py:350
  2.5 1.6 %collective-permute-start.3 = (bf16[2,256,128]{2,1,0:T(8,128)(2,1)}, bf16[2,256,128]{2,1,0:T(8,128)(2,1)S(1)}, u32[]{:S(2)}, u32[]{:S(2)}) collective-permute-start(bf16[2,256,128]{2,1,0:T(8,128)(2,1)} %get-tuple-element.27), channel_id=1, source_target_pairs={{0,8},{2,10},{4,12},{6,14},{8,0},{10,2},{12,4},{14,6},{1,9},{3,11}... | collective-permute-start | bytes 393224 | tf_op jit(solution)/shard_map/ppermute | solution.py:369
  4.0 1.5 %collective-permute-start.4 = (bf16[2,256,128]{2,1,0:T(8,128)(2,1)}, bf16[2,256,128]{2,1,0:T(8,128)(2,1)S(1)}, u32[]{:S(2)}, u32[]{:S(2)}) collective-permute-start(bf16[2,256,128]{2,1,0:T(8,128)(2,1)} %get-tuple-element.28), channel_id=1, source_target_pairs={{0,10},{2,8},{4,14},{6,12},{8,2},{10,0},{12,6},{14,4},{1,11},{3,9}... | collective-permute-start | bytes 393224 | tf_op jit(solution)/shard_map/ppermute | solution.py:369
  5.6 3.8 %collective-permute-start.5 = (bf16[2,256,128]{2,1,0:T(8,128)(2,1)}, bf16[2,256,128]{2,1,0:T(8,128)(2,1)S(1)}, u32[]{:S(2)}, u32[]{:S(2)}) collective-permute-start(bf16[2,256,128]{2,1,0:T(8,128)(2,1)} %get-tuple-element.29), channel_id=1, source_target_pairs={{0,12},{2,14},{4,8},{6,10},{8,4},{10,6},{12,0},{14,2},{1,13},{3,15... | collective-permute-start | bytes 393224 | tf_op jit(solution)/shard_map/ppermute | solution.py:369
  10.0 4.3 %collective-permute-done.refs_1_ = bf16[80,128]{1,0:T(8,128)(2,1)S(1)} collective-permute-done((bf16[80,128]{1,0:T(8,128)(2,1)}, bf16[80,128]{1,0:T(8,128)(2,1)S(1)}, u32[]{:S(2)}, u32[]{:S(2)}) %collective-permute-start) | collective-permute-done | bytes 20512 | tf_op jit(solution)/shard_map/ppermute | solution.py:347
  14.3 2.9 %collective-permute-start.1 = (bf16[80,128]{1,0:T(8,128)(2,1)}, bf16[80,128]{1,0:T(8,128)(2,1)S(1)}, u32[]{:S(2)}, u32[]{:S(2)}) collective-permute-start(bf16[80,128]{1,0:T(8,128)(2,1)} %get-tuple-element.25), channel_id=1, source_target_pairs={{0,4},{2,6},{4,0},{6,2},{1,5},{3,7},{5,1},{7,3},{8,12},{10,14},{12... | collective-permute-start | bytes 61448 | tf_op jit(solution)/shard_map/ppermute | solution.py:347
  17.2 2.6 %collective-permute-done.1.refs_2_ = bf16[80,128]{1,0:T(8,128)(2,1)S(1)} collective-permute-done((bf16[80,128]{1,0:T(8,128)(2,1)}, bf16[80,128]{1,0:T(8,128)(2,1)S(1)}, u32[]{:S(2)}, u32[]{:S(2)}) %collective-permute-start.1) | collective-permute-done | bytes 20512 | tf_op jit(solution)/shard_map/ppermute | solution.py:347
  19.8 2.5 %collective-permute-start.2 = (bf16[80,128]{1,0:T(8,128)(2,1)}, bf16[80,128]{1,0:T(8,128)(2,1)S(1)}, u32[]{:S(2)}, u32[]{:S(2)}) collective-permute-start(bf16[80,128]{1,0:T(8,128)(2,1)} %get-tuple-element.26), channel_id=1, source_target_pairs={{0,6},{2,4},{4,2},{6,0},{1,7},{3,5},{5,3},{7,1},{8,14},{10,12},{12... | collective-permute-start | bytes 61448 | tf_op jit(solution)/shard_map/ppermute | solution.py:347
  22.3 2.7 %collective-permute-done.2.refs_3_ = bf16[80,128]{1,0:T(8,128)(2,1)S(1)} collective-permute-done((bf16[80,128]{1,0:T(8,128)(2,1)}, bf16[80,128]{1,0:T(8,128)(2,1)S(1)}, u32[]{:S(2)}, u32[]{:S(2)}) %collective-permute-start.2) | collective-permute-done | bytes 20512 | tf_op jit(solution)/shard_map/ppermute | solution.py:347
  25.1 0.7 copy-done.7
  25.8 1.5 %pack.1 = bf16[2048,128]{1,0:T(8,128)(2,1)} custom-call(s32[1]{0:T(128)} %bitcast.place_ref, bf16[80,128]{1,0:T(8,128)(2,1)S(1)} %copy-done.7, bf16[80,128]{1,0:T(8,128)(2,1)S(1)} %collective-permute-done.refs_1_, bf16[80,128]{1,0:T(8,128)(2,1)S(1)} %collective-permute-done.1.refs_2_, bf16[80,128]{1,0:T(8,128)(2,1)S(1)} %collective-permute-done.2.refs_3_, ...), custom_call_target="tpu_custom_call" | custom-call | tf_op jit(solution)/shard_map/pack/pallas_call | solution.py:399
  27.3 11.2 %all-to-all-start = ((bf16[32,64,128]{2,1,0:T(8,128)(2,1)}), bf16[32,64,128]{2,1,0:T(8,128)(2,1)S(1)}, u32[]{:S(2)}, u32[]{:S(2)}) async-start(bf16[32,64,128]{2,1,0:T(8,128)(2,1)} %bitcast.1), calls=%async_computation | async-start | bytes 1048576 | tf_op jit(solution)/shard_map/all_to_all | solution.py:407
  38.6 4.0 %collective-permute-start.8 = (bf16[2,256,128]{2,1,0:T(8,128)(2,1)S(1)}, bf16[2,256,128]{2,1,0:T(8,128)(2,1)S(1)}, u32[]{:S(2)}, u32[]{:S(2)}) collective-permute-start(bf16[2,256,128]{2,1,0:T(8,128)(2,1)S(1)} %copy-done.26), channel_id=1, source_target_pairs={{0,4},{2,6},{4,0},{6,2},{8,12},{10,14},{12,8},{14,10},{1,5},{3,7},... | collective-permute-start | bytes 393224 | tf_op jit(solution)/shard_map/ppermute | solution.py:369
  42.6 0.7 collective-permute-start.9
  43.3 0.5 collective-permute-start.14
  43.9 3.0 %collective-permute-done.8.refs_2_ = bf16[2,256,128]{2,1,0:T(8,128)(2,1)S(1)} collective-permute-done((bf16[2,256,128]{2,1,0:T(8,128)(2,1)S(1)}, bf16[2,256,128]{2,1,0:T(8,128)(2,1)S(1)}, u32[]{:S(2)}, u32[]{:S(2)}) %collective-permute-start.8) | collective-permute-done | bytes 131104 | tf_op jit(solution)/shard_map/ppermute | solution.py:369
  47.0 1.8 %collective-permute-done.9.refs_3_ = bf16[2,256,128]{2,1,0:T(8,128)(2,1)S(1)} collective-permute-done((bf16[2,256,128]{2,1,0:T(8,128)(2,1)S(1)}, bf16[2,256,128]{2,1,0:T(8,128)(2,1)S(1)}, u32[]{:S(2)}, u32[]{:S(2)}) %collective-permute-start.9) | collective-permute-done | bytes 131104 | tf_op jit(solution)/shard_map/ppermute | solution.py:369
  48.8 0.5 collective-permute-start.11
  49.4 0.4 collective-permute-start.13
  51.0 4.0 %all-to-all-done = bf16[32,64,128]{2,1,0:T(8,128)(2,1)S(1)} async-done(((bf16[32,64,128]{2,1,0:T(8,128)(2,1)}), bf16[32,64,128]{2,1,0:T(8,128)(2,1)S(1)}, u32[]{:S(2)}, u32[]{:S(2)}) %all-to-all-start) | async-done | bytes 524320 | tf_op jit(solution)/shard_map/all_to_all | solution.py:407
  55.1 0.7 copy-done.12
  55.9 6.3 %far.1 = bf16[32,80,128]{2,1,0:T(8,128)(2,1)} custom-call(bf16[2048,128]{1,0:T(8,128)(2,1)} %bitcast.3, bf16[2,256,128]{2,1,0:T(8,128)(2,1)} %get-tuple-element.31.refs_0_, bf16[2,256,128]{2,1,0:T(8,128)(2,1)} %copy-done.14, bf16[2,256,128]{2,1,0:T(8,128)(2,1)} %copy-done.15, bf16[2,256,128]{2,1,0:T(8,128)(2,1)} %copy-done.16, ...), custom_call_target="tpu_custom_call" | custom-call | tf_op jit(solution)/shard_map/far/pallas_call | solution.py:409
  62.2 9.7 %all-to-all-start.1 = ((bf16[32,80,128]{2,1,0:T(8,128)(2,1)}), bf16[32,80,128]{2,1,0:T(8,128)(2,1)S(1)}, u32[]{:S(2)}, u32[]{:S(2)}) async-start(bf16[32,80,128]{2,1,0:T(8,128)(2,1)} %far.1), calls=%async_computation.1 | async-start | bytes 1310720 | tf_op jit(solution)/shard_map/all_to_all | solution.py:425
  72.0 1.6 %copy-done.1 = bf16[8,256,512]{2,1,0:T(8,128)(2,1)S(1)} copy-done((bf16[8,256,512]{2,1,0:T(8,128)(2,1)S(1)}, bf16[8,256,512]{2,1,0:T(8,128)(2,1)}, u32[]{:S(2)}) %copy-start.1) | copy-done | bytes 2097176
  73.5 4.0 %near.1 = (f32[32,8,128]{2,1,0:T(8,128)S(1)}, f32[32,8,128]{2,1,0:T(8,128)S(1)}) custom-call(s32[8]{0:T(128)S(1)} %copy-done.11, bf16[8,4096]{1,0:T(8,128)(2,1)S(1)} %copy-done.6, bf16[8,512]{1,0:T(8,128)(2,1)S(1)} %copy-done.9, bf16[8,512]{1,0:T(8,128)(2,1)S(1)} %copy-done.10, bf16[8,256,512]{2,1,0:T(8,128)(2,1)S(1)} %copy-done, ...), custom_call_target="tpu_custom_call" | custom-call | flops 300000000 | bytes 4500000 | tf_op jit(solution)/shard_map/near/pallas_call | solution.py:372
  77.5 13.7 %all-to-all-done.1.back_ref = bf16[32,80,128]{2,1,0:T(8,128)(2,1)S(1)} async-done(((bf16[32,80,128]{2,1,0:T(8,128)(2,1)}), bf16[32,80,128]{2,1,0:T(8,128)(2,1)S(1)}, u32[]{:S(2)}, u32[]{:S(2)}) %all-to-all-start.1) | async-done | bytes 655392 | tf_op jit(solution)/shard_map/all_to_all | solution.py:425
  91.2 0.5 select.1
  91.8 2.2 %collective-permute-start.19 = (bf16[80,128]{1,0:T(8,128)(2,1)S(1)}, bf16[80,128]{1,0:T(8,128)(2,1)S(1)}, u32[]{:S(2)}, u32[]{:S(2)}) collective-permute-start(bf16[80,128]{1,0:T(8,128)(2,1)S(1)} %get-tuple-element.39), channel_id=1, source_target_pairs={{0,4},{2,6},{4,0},{6,2},{1,5},{3,7},{5,1},{7,3},{8,12},{10,14},{12... | collective-permute-start | bytes 61448 | tf_op jit(solution)/shard_map/ppermute | solution.py:347
  94.0 2.5 %collective-permute-start.20 = (bf16[80,128]{1,0:T(8,128)(2,1)S(1)}, bf16[80,128]{1,0:T(8,128)(2,1)S(1)}, u32[]{:S(2)}, u32[]{:S(2)}) collective-permute-start(bf16[80,128]{1,0:T(8,128)(2,1)S(1)} %get-tuple-element.40), channel_id=1, source_target_pairs={{0,6},{2,4},{4,2},{6,0},{1,7},{3,5},{5,3},{7,1},{8,14},{10,12},{12... | collective-permute-start | bytes 61448 | tf_op jit(solution)/shard_map/ppermute | solution.py:347
  96.5 0.7 collective-permute-done.19.refs_2_
  97.2 1.8 %collective-permute-done.20.refs_3_ = bf16[80,128]{1,0:T(8,128)(2,1)S(1)} collective-permute-done((bf16[80,128]{1,0:T(8,128)(2,1)S(1)}, bf16[80,128]{1,0:T(8,128)(2,1)S(1)}, u32[]{:S(2)}, u32[]{:S(2)}) %collective-permute-start.20) | collective-permute-done | bytes 20512 | tf_op jit(solution)/shard_map/ppermute | solution.py:347
  99.0 0.8 merge.1
  (76 shorter events, 2.2 us)
Async XLA Ops:
  2.5 22.6 %collective-permute-start.3 = (bf16[2,256,128]{2,1,0:T(8,128)(2,1)}, bf16[2,256,128]{2,1,0:T(8,128)(2,1)S(1)}, u32[]{:S(2)}, u32[]{:S(2)}) collective-permute-start(bf16[2,256,128]{2,1,0:T(8,128)(2,1)} %get-tuple-element.27), channel_id=1, source_target_pairs={{0,8},{2,10},{4,12},{6,14},{8,0},{10,2},{12,4},{14,6},{1,9},{3,11}... | collective-permute-start | bytes 393224 | tf_op jit(solution)/shard_map/ppermute | solution.py:369
  4.0 21.0 %collective-permute-start.4 = (bf16[2,256,128]{2,1,0:T(8,128)(2,1)}, bf16[2,256,128]{2,1,0:T(8,128)(2,1)S(1)}, u32[]{:S(2)}, u32[]{:S(2)}) collective-permute-start(bf16[2,256,128]{2,1,0:T(8,128)(2,1)} %get-tuple-element.28), channel_id=1, source_target_pairs={{0,10},{2,8},{4,14},{6,12},{8,2},{10,0},{12,6},{14,4},{1,11},{3,9}... | collective-permute-start | bytes 393224 | tf_op jit(solution)/shard_map/ppermute | solution.py:369
  5.6 19.4 %collective-permute-start.5 = (bf16[2,256,128]{2,1,0:T(8,128)(2,1)}, bf16[2,256,128]{2,1,0:T(8,128)(2,1)S(1)}, u32[]{:S(2)}, u32[]{:S(2)}) collective-permute-start(bf16[2,256,128]{2,1,0:T(8,128)(2,1)} %get-tuple-element.29), channel_id=1, source_target_pairs={{0,12},{2,14},{4,8},{6,10},{8,4},{10,6},{12,0},{14,2},{1,13},{3,15... | collective-permute-start | bytes 393224 | tf_op jit(solution)/shard_map/ppermute | solution.py:369
  9.4 15.6 %collective-permute-start.6 = (bf16[2,256,128]{2,1,0:T(8,128)(2,1)}, bf16[2,256,128]{2,1,0:T(8,128)(2,1)S(1)}, u32[]{:S(2)}, u32[]{:S(2)}) collective-permute-start(bf16[2,256,128]{2,1,0:T(8,128)(2,1)} %get-tuple-element.30), channel_id=1, source_target_pairs={{0,14},{2,12},{4,10},{6,8},{8,6},{10,4},{12,2},{14,0},{1,15},{3,13... | collective-permute-start | bytes 393224 | tf_op jit(solution)/shard_map/ppermute | solution.py:369
  9.6 4.7 %collective-permute-start = (bf16[80,128]{1,0:T(8,128)(2,1)}, bf16[80,128]{1,0:T(8,128)(2,1)S(1)}, u32[]{:S(2)}, u32[]{:S(2)}) collective-permute-start(bf16[80,128]{1,0:T(8,128)(2,1)} %get-tuple-element.24), channel_id=1, source_target_pairs={{0,2},{2,0},{4,6},{6,4},{1,3},{3,1},{5,7},{7,5},{8,10},{10,8},{12,... | collective-permute-start | bytes 61448 | tf_op jit(solution)/shard_map/ppermute | solution.py:347
  14.3 5.5 %collective-permute-start.1 = (bf16[80,128]{1,0:T(8,128)(2,1)}, bf16[80,128]{1,0:T(8,128)(2,1)S(1)}, u32[]{:S(2)}, u32[]{:S(2)}) collective-permute-start(bf16[80,128]{1,0:T(8,128)(2,1)} %get-tuple-element.25), channel_id=1, source_target_pairs={{0,4},{2,6},{4,0},{6,2},{1,5},{3,7},{5,1},{7,3},{8,12},{10,14},{12... | collective-permute-start | bytes 61448 | tf_op jit(solution)/shard_map/ppermute | solution.py:347
  19.8 5.2 %collective-permute-start.2 = (bf16[80,128]{1,0:T(8,128)(2,1)}, bf16[80,128]{1,0:T(8,128)(2,1)S(1)}, u32[]{:S(2)}, u32[]{:S(2)}) collective-permute-start(bf16[80,128]{1,0:T(8,128)(2,1)} %get-tuple-element.26), channel_id=1, source_target_pairs={{0,6},{2,4},{4,2},{6,0},{1,7},{3,5},{5,3},{7,1},{8,14},{10,12},{12... | collective-permute-start | bytes 61448 | tf_op jit(solution)/shard_map/ppermute | solution.py:347
  25.0 30.1 %copy-start.2 = (bf16[2,256,128]{2,1,0:T(8,128)(2,1)}, bf16[2,256,128]{2,1,0:T(8,128)(2,1)S(1)}, u32[]{:S(2)}) copy-start(bf16[2,256,128]{2,1,0:T(8,128)(2,1)S(1)} %collective-permute-done.3.refs_4_) | copy-start | bytes 393220
  25.0 30.1 %copy-start.3 = (bf16[2,256,128]{2,1,0:T(8,128)(2,1)}, bf16[2,256,128]{2,1,0:T(8,128)(2,1)S(1)}, u32[]{:S(2)}) copy-start(bf16[2,256,128]{2,1,0:T(8,128)(2,1)S(1)} %collective-permute-done.4.refs_5_) | copy-start | bytes 393220
  25.0 30.1 %copy-start.4 = (bf16[2,256,128]{2,1,0:T(8,128)(2,1)}, bf16[2,256,128]{2,1,0:T(8,128)(2,1)S(1)}, u32[]{:S(2)}) copy-start(bf16[2,256,128]{2,1,0:T(8,128)(2,1)S(1)} %collective-permute-done.5.refs_6_) | copy-start | bytes 393220
  25.1 30.0 %copy-start.5 = (bf16[2,256,128]{2,1,0:T(8,128)(2,1)}, bf16[2,256,128]{2,1,0:T(8,128)(2,1)S(1)}, u32[]{:S(2)}) copy-start(bf16[2,256,128]{2,1,0:T(8,128)(2,1)S(1)} %collective-permute-done.6.refs_7_) | copy-start | bytes 393220
  25.8 16.8 %copy-start.25 = (bf16[2,256,128]{2,1,0:T(8,128)(2,1)S(1)}, bf16[2,256,128]{2,1,0:T(8,128)(2,1)}, u32[]{:S(2)}) copy-start(bf16[2,256,128]{2,1,0:T(8,128)(2,1)} %get-tuple-element.34) | copy-start | bytes 393220
  25.8 17.5 %copy-start.13 = (bf16[2,256,128]{2,1,0:T(8,128)(2,1)S(1)}, bf16[2,256,128]{2,1,0:T(8,128)(2,1)}, u32[]{:S(2)}) copy-start(bf16[2,256,128]{2,1,0:T(8,128)(2,1)} %get-tuple-element.31.refs_0_) | copy-start | bytes 393220
  27.3 27.7 %all-to-all-start = ((bf16[32,64,128]{2,1,0:T(8,128)(2,1)}), bf16[32,64,128]{2,1,0:T(8,128)(2,1)S(1)}, u32[]{:S(2)}, u32[]{:S(2)}) async-start(bf16[32,64,128]{2,1,0:T(8,128)(2,1)} %bitcast.1), calls=%async_computation | async-start | bytes 1048576 | tf_op jit(solution)/shard_map/all_to_all | solution.py:407
  38.5 5.3 %collective-permute-start.7 = (bf16[2,256,128]{2,1,0:T(8,128)(2,1)S(1)}, bf16[2,256,128]{2,1,0:T(8,128)(2,1)S(1)}, u32[]{:S(2)}, u32[]{:S(2)}) collective-permute-start(bf16[2,256,128]{2,1,0:T(8,128)(2,1)S(1)} %copy-done.27), channel_id=1, source_target_pairs={{0,2},{2,0},{4,6},{6,4},{8,10},{10,8},{12,14},{14,12},{1,3},{3,1},... | collective-permute-start | bytes 393224 | tf_op jit(solution)/shard_map/ppermute | solution.py:369
  38.6 8.3 %collective-permute-start.8 = (bf16[2,256,128]{2,1,0:T(8,128)(2,1)S(1)}, bf16[2,256,128]{2,1,0:T(8,128)(2,1)S(1)}, u32[]{:S(2)}, u32[]{:S(2)}) collective-permute-start(bf16[2,256,128]{2,1,0:T(8,128)(2,1)S(1)} %copy-done.26), channel_id=1, source_target_pairs={{0,4},{2,6},{4,0},{6,2},{8,12},{10,14},{12,8},{14,10},{1,5},{3,7},... | collective-permute-start | bytes 393224 | tf_op jit(solution)/shard_map/ppermute | solution.py:369
  42.6 6.2 %collective-permute-start.9 = (bf16[2,256,128]{2,1,0:T(8,128)(2,1)S(1)}, bf16[2,256,128]{2,1,0:T(8,128)(2,1)S(1)}, u32[]{:S(2)}, u32[]{:S(2)}) collective-permute-start(bf16[2,256,128]{2,1,0:T(8,128)(2,1)S(1)} %copy-done.25), channel_id=1, source_target_pairs={{0,6},{2,4},{4,2},{6,0},{8,14},{10,12},{12,10},{14,8},{1,7},{3,5},... | collective-permute-start | bytes 393224 | tf_op jit(solution)/shard_map/ppermute | solution.py:369
  43.3 5.5 %collective-permute-start.10 = (bf16[2,256,128]{2,1,0:T(8,128)(2,1)S(1)}, bf16[2,256,128]{2,1,0:T(8,128)(2,1)S(1)}, u32[]{:S(2)}, u32[]{:S(2)}) collective-permute-start(bf16[2,256,128]{2,1,0:T(8,128)(2,1)S(1)} %copy-done.13), channel_id=1, source_target_pairs={{0,1},{1,0},{2,3},{3,2},{4,5},{5,4},{6,7},{7,6},{8,9},{9,8},{10,11... | collective-permute-start | bytes 393224 | tf_op jit(solution)/shard_map/ppermute | solution.py:370
  43.3 6.0 %collective-permute-start.14 = (bf16[2,256,128]{2,1,0:T(8,128)(2,1)S(1)}, bf16[2,256,128]{2,1,0:T(8,128)(2,1)S(1)}, u32[]{:S(2)}, u32[]{:S(2)}) collective-permute-start(bf16[2,256,128]{2,1,0:T(8,128)(2,1)S(1)} %collective-permute-done.3.refs_4_), channel_id=1, source_target_pairs={{0,1},{1,0},{2,3},{3,2},{4,5},{5,4},{6,7},{7,6},{8,9},{9,8},{10,11... | collective-permute-start | bytes 393224 | tf_op jit(solution)/shard_map/ppermute | solution.py:370
  43.8 5.6 %collective-permute-start.15 = (bf16[2,256,128]{2,1,0:T(8,128)(2,1)S(1)}, bf16[2,256,128]{2,1,0:T(8,128)(2,1)S(1)}, u32[]{:S(2)}, u32[]{:S(2)}) collective-permute-start(bf16[2,256,128]{2,1,0:T(8,128)(2,1)S(1)} %collective-permute-done.4.refs_5_), channel_id=1, source_target_pairs={{0,1},{1,0},{2,3},{3,2},{4,5},{5,4},{6,7},{7,6},{8,9},{9,8},{10,11... | collective-permute-start | bytes 393224 | tf_op jit(solution)/shard_map/ppermute | solution.py:370
  46.9 2.9 %collective-permute-start.16 = (bf16[2,256,128]{2,1,0:T(8,128)(2,1)S(1)}, bf16[2,256,128]{2,1,0:T(8,128)(2,1)S(1)}, u32[]{:S(2)}, u32[]{:S(2)}) collective-permute-start(bf16[2,256,128]{2,1,0:T(8,128)(2,1)S(1)} %collective-permute-done.5.refs_6_), channel_id=1, source_target_pairs={{0,1},{1,0},{2,3},{3,2},{4,5},{5,4},{6,7},{7,6},{8,9},{9,8},{10,11... | collective-permute-start | bytes 393224 | tf_op jit(solution)/shard_map/ppermute | solution.py:370
  48.8 1.3 %collective-permute-start.17 = (bf16[2,256,128]{2,1,0:T(8,128)(2,1)S(1)}, bf16[2,256,128]{2,1,0:T(8,128)(2,1)S(1)}, u32[]{:S(2)}, u32[]{:S(2)}) collective-permute-start(bf16[2,256,128]{2,1,0:T(8,128)(2,1)S(1)} %collective-permute-done.6.refs_7_), channel_id=1, source_target_pairs={{0,1},{1,0},{2,3},{3,2},{4,5},{5,4},{6,7},{7,6},{8,9},{9,8},{10,11... | collective-permute-start | bytes 393224 | tf_op jit(solution)/shard_map/ppermute | solution.py:370
  48.8 1.5 %collective-permute-start.11 = (bf16[2,256,128]{2,1,0:T(8,128)(2,1)S(1)}, bf16[2,256,128]{2,1,0:T(8,128)(2,1)S(1)}, u32[]{:S(2)}, u32[]{:S(2)}) collective-permute-start(bf16[2,256,128]{2,1,0:T(8,128)(2,1)S(1)} %collective-permute-done.7.refs_1_), channel_id=1, source_target_pairs={{0,1},{1,0},{2,3},{3,2},{4,5},{5,4},{6,7},{7,6},{8,9},{9,8},{10,11... | collective-permute-start | bytes 393224 | tf_op jit(solution)/shard_map/ppermute | solution.py:370
  49.3 1.3 %collective-permute-start.12 = (bf16[2,256,128]{2,1,0:T(8,128)(2,1)S(1)}, bf16[2,256,128]{2,1,0:T(8,128)(2,1)S(1)}, u32[]{:S(2)}, u32[]{:S(2)}) collective-permute-start(bf16[2,256,128]{2,1,0:T(8,128)(2,1)S(1)} %collective-permute-done.8.refs_2_), channel_id=1, source_target_pairs={{0,1},{1,0},{2,3},{3,2},{4,5},{5,4},{6,7},{7,6},{8,9},{9,8},{10,11... | collective-permute-start | bytes 393224 | tf_op jit(solution)/shard_map/ppermute | solution.py:370
  49.4 1.5 %collective-permute-start.13 = (bf16[2,256,128]{2,1,0:T(8,128)(2,1)S(1)}, bf16[2,256,128]{2,1,0:T(8,128)(2,1)S(1)}, u32[]{:S(2)}, u32[]{:S(2)}) collective-permute-start(bf16[2,256,128]{2,1,0:T(8,128)(2,1)S(1)} %collective-permute-done.9.refs_3_), channel_id=1, source_target_pairs={{0,1},{1,0},{2,3},{3,2},{4,5},{5,4},{6,7},{7,6},{8,9},{9,8},{10,11... | collective-permute-start | bytes 393224 | tf_op jit(solution)/shard_map/ppermute | solution.py:370
  55.9 16.1 %copy-start.10 = (bf16[8,512]{1,0:T(8,128)(2,1)S(1)}, bf16[8,512]{1,0:T(8,128)(2,1)}, u32[]{:S(2)}) copy-start(bf16[8,512]{1,0:T(8,128)(2,1)} %new_value_ref.1) | copy-start | bytes 24580
  55.9 16.1 %copy-start.11 = (s32[8]{0:T(128)S(1)}, s32[8]{0:T(128)}, u32[]{:S(2)}) copy-start(s32[8]{0:T(128)} %len_ref.1) | copy-start | bytes 100
  62.2 29.1 %all-to-all-start.1 = ((bf16[32,80,128]{2,1,0:T(8,128)(2,1)}), bf16[32,80,128]{2,1,0:T(8,128)(2,1)S(1)}, u32[]{:S(2)}, u32[]{:S(2)}) async-start(bf16[32,80,128]{2,1,0:T(8,128)(2,1)} %far.1), calls=%async_computation.1 | async-start | bytes 1310720 | tf_op jit(solution)/shard_map/all_to_all | solution.py:425
  73.5 17.7 %copy-start.8 = (bf16[80,128]{1,0:T(8,128)(2,1)S(1)}, bf16[80,128]{1,0:T(8,128)(2,1)}, u32[]{:S(2)}) copy-start(bf16[80,128]{1,0:T(8,128)(2,1)} %get-tuple-element.23.refs_0_) | copy-start | bytes 61444
  91.7 4.8 %collective-permute-start.18 = (bf16[80,128]{1,0:T(8,128)(2,1)S(1)}, bf16[80,128]{1,0:T(8,128)(2,1)S(1)}, u32[]{:S(2)}, u32[]{:S(2)}) collective-permute-start(bf16[80,128]{1,0:T(8,128)(2,1)S(1)} %get-tuple-element.38), channel_id=1, source_target_pairs={{0,2},{2,0},{4,6},{6,4},{1,3},{3,1},{5,7},{7,5},{8,10},{10,8},{12,... | collective-permute-start | bytes 61448 | tf_op jit(solution)/shard_map/ppermute | solution.py:347
  91.8 5.4 %collective-permute-start.19 = (bf16[80,128]{1,0:T(8,128)(2,1)S(1)}, bf16[80,128]{1,0:T(8,128)(2,1)S(1)}, u32[]{:S(2)}, u32[]{:S(2)}) collective-permute-start(bf16[80,128]{1,0:T(8,128)(2,1)S(1)} %get-tuple-element.39), channel_id=1, source_target_pairs={{0,4},{2,6},{4,0},{6,2},{1,5},{3,7},{5,1},{7,3},{8,12},{10,14},{12... | collective-permute-start | bytes 61448 | tf_op jit(solution)/shard_map/ppermute | solution.py:347
  94.0 5.0 %collective-permute-start.20 = (bf16[80,128]{1,0:T(8,128)(2,1)S(1)}, bf16[80,128]{1,0:T(8,128)(2,1)S(1)}, u32[]{:S(2)}, u32[]{:S(2)}) collective-permute-start(bf16[80,128]{1,0:T(8,128)(2,1)S(1)} %get-tuple-element.40), channel_id=1, source_target_pairs={{0,6},{2,4},{4,2},{6,0},{1,7},{3,5},{5,3},{7,1},{8,14},{10,12},{12... | collective-permute-start | bytes 61448 | tf_op jit(solution)/shard_map/ppermute | solution.py:347
  (19 other events, 143.1 us)
